TPU v7x, 32 devices: a whole 2x2x4 slice. The times are simulated.
32 devices in a mesh: tile: 8 (over z, y), vec: 4 (over x, core).
Axes of the slice: x: 2, y: 2, z: 4, core: 2. Of those that a mesh axis runs over, the one named last changes fastest.
Arguments:
- vectors: float32 [64, 16, 32, 128], P('vec', 'tile'), may hold values from -6 to 6
- previous: float32 [64, 16, 32, 128], P('vec', 'tile'), may hold values from -3 to 3
- intensity: float32 [16, 32, 128], P('tile'), may hold values from 0 to 2
- counts: int32 [8], P('tile'), may hold values from 0 to 8192
- coef_x: bfloat16 [3, 64, 64], replicated, may hold values from -0.4375 to 0.4375
- coef_p: bfloat16 [2, 64, 64], replicated, may hold values from -0.5 to 0.5
Outputs:
- x_next: float32 [64, 16, 32, 128], P('vec', 'tile')
- p_next: float32 [64, 16, 32, 128], P('vec', 'tile')
- residual_image: float32 [64, 16, 32, 128], P('vec', 'tile')
- gram_s: float32 [3, 64, 3, 64], P(None, 'vec')
- gram_a: float32 [3, 64, 3, 64], P(None, 'vec')
All inputs are finite; a program needn't handle non-finite values.
Results may differ from a plain program's by a relative error of at most 0.0029.
Values may be sent and summed in bfloat16 or wider, within the bound.
A program may use at most 64 MiB of HBM per device.

v0:
```python
import jax
import jax.numpy as jnp
from jax import lax
from jax.sharding import PartitionSpec as P

offsets = ((1, 0, 0), (-1, 0, 0), (0, 1, 0), (0, -1, 0), (0, 0, 1), (0, 0, -1))


def with_halo(value, sides, width):
    for axis, dim in sides:
        count, length = (lax.axis_size(axis), value.shape[dim])
        up = [(i, (i + 1) % count) for i in range(count - 1)]
        down = [(j, i) for i, j in up]
        last = lax.slice_in_dim(value, length - width, length, axis=dim)
        first = lax.slice_in_dim(value, 0, width, axis=dim)
        before = lax.ppermute(last, axis, up)
        after = lax.ppermute(first, axis, down)
        value = jnp.concatenate([before, value, after], axis=dim)
    return value


def pick(padded, offset, shape):
    dx, dy, dz = offset
    return padded[
        ..., 1 + dx : 1 + dx + shape[0], 1 + dy : 1 + dy + shape[1], 1 + dz : 1 + dz + shape[2]
    ]


def graph(image_pad, weight_pad, shape):
    centre = pick(image_pad, (0, 0, 0), shape)
    gcentre = pick(weight_pad, (0, 0, 0), shape)
    weights = [
        jnp.exp(-((centre - pick(image_pad, o, shape)) ** 2)) * gcentre * pick(weight_pad, o, shape)
        for o in offsets
    ]
    degree = weights[0]
    for w in weights[1:]:
        degree = degree + w
    return (weights, lax.rsqrt(degree))


def apply_op(field, weights, inv, pad_fn, shape):
    padded = pad_fn(field * inv)
    total = weights[0] * pick(padded, offsets[0], shape)
    for w, o in zip(weights[1:], offsets[1:]):
        total = total + w * pick(padded, o, shape)
    return field - inv * total


def side_pad(padded):
    return jnp.pad(padded, ((0, 0), (0, 0), (1, 1), (1, 1)))


def pad_vectors(u):
    return side_pad(with_halo(u, (("tile", 1),), 1))


def pad_residual(u):
    return side_pad(with_halo(u, (("tile", 1),), 1))


def shards(vectors, previous, intensity, counts, coef_x, coef_p):
    ncols, cx, cy, cz = vectors.shape
    shape = (cx, cy, cz)
    nloc = cx * cy * cz
    ix = lax.broadcasted_iota(jnp.int32, shape, 0)
    iy = lax.broadcasted_iota(jnp.int32, shape, 1)
    iz = lax.broadcasted_iota(jnp.int32, shape, 2)
    lin = (ix * cy + iy) * cz + iz
    gvals = jnp.where(lin < counts[0], 1.0, 0.0).astype(jnp.float32) * 0.9 + 0.1
    stacked = jnp.stack([intensity, gvals])
    padded = side_pad(with_halo(stacked, (("tile", 1),), 1))
    weights, inv = graph(padded[0], padded[1], shape)
    both = apply_op(jnp.concatenate([vectors, previous], axis=0), weights, inv, pad_vectors, shape)
    ax_img = both[:ncols]
    ap_img = both[ncols:]
    num = jnp.sum(vectors * ax_img, axis=(1, 2, 3))
    den = jnp.sum(vectors * vectors, axis=(1, 2, 3))
    num, den = lax.psum((num, den), "tile")
    lam = (num / den)[:, None, None, None]
    resid = ax_img - lam * vectors
    ar_img = apply_op(resid, weights, inv, pad_residual, shape)
    basis = jnp.stack([vectors, resid, previous]).astype(jnp.bfloat16).reshape(3, ncols, nloc)
    images = jnp.stack([ax_img, ar_img, ap_img]).astype(jnp.bfloat16).reshape(3, ncols, nloc)
    nvox = nloc * lax.axis_size("tile")
    start = lax.axis_index("vec") * ncols
    whole = lax.all_gather(basis, "vec", axis=1, tiled=True)
    gram_s = jnp.einsum("aiv,bjv->aibj", basis, whole, preferred_element_type=jnp.float32)
    gram_a = jnp.einsum("aiv,bjv->aibj", images, whole, preferred_element_type=jnp.float32)
    gram_s, gram_a = lax.psum((gram_s, gram_a), "tile")
    gram_s = gram_s / nvox
    gram_a = gram_a / nvox
    own_x = lax.dynamic_slice_in_dim(coef_x, start, ncols, 2)
    own_p = lax.dynamic_slice_in_dim(coef_p, start, ncols, 2)
    x_next = jnp.einsum("aiv,aij->jv", whole, own_x, preferred_element_type=jnp.float32)
    p_next = jnp.einsum("aiv,aij->jv", whole[1:], own_p, preferred_element_type=jnp.float32)
    return (
        x_next.reshape(ncols, cx, cy, cz),
        p_next.reshape(ncols, cx, cy, cz),
        ar_img,
        gram_s,
        gram_a,
    )


def solution(mesh):
    placed = (
        P("vec", "tile", None, None),
        P("vec", "tile", None, None),
        P("tile", None, None),
        P("tile"),
        P(),
        P(),
    )
    return jax.shard_map(
        shards,
        mesh=mesh,
        in_specs=placed,
        out_specs=(
            P("vec", "tile", None, None),
            P("vec", "tile", None, None),
            P("vec", "tile", None, None),
            P(None, "vec", None, None),
            P(None, "vec", None, None),
        ),
        check_vma=False,
    )
```

profile of v0, /device:TPU:0, one launch (start us, length us, event | category | flops | bytes accessed | tf_op | source)
XLA Modules:
  0.0 205.3 jit_solution(15681022785362163921)
XLA Ops:
  7.9 0.1 multiply_add_fusion
  8.0 0.7 fusion.42
  8.7 4.9 %collective-permute-start = (f32[2,1,32,128]{3,2,1,0:T(8,128)S(1)}, f32[2,1,32,128]{3,2,1,0:T(8,128)S(1)}, u32[]{:S(2)}, u32[]{:S(2)}) collective-permute-start(f32[2,1,32,128]{3,2,1,0:T(8,128)S(1)} %get-tuple-element.34), channel_id=1, source_target_pairs={{0,4},{4,8},{8,12},{12,16},{16,20},{20,24},{24,28},{1,5},{5,9},{9,... | collective-permute-start | bytes 98312 | tf_op jit(solution)/shard_map/ppermute | solution.py:16
  13.6 1.3 collective-permute-start.1
  14.9 1.1 constant_dynamic-update-slice_fusion.1
  16.0 1.3 fusion.76
  17.3 2.1 %collective-permute-done.1 = f32[2,1,32,128]{3,2,1,0:T(8,128)S(1)} collective-permute-done((f32[2,1,32,128]{3,2,1,0:T(8,128)S(1)}, f32[2,1,32,128]{3,2,1,0:T(8,128)S(1)}, u32[]{:S(2)}, u32[]{:S(2)}) %collective-permute-start.1) | collective-permute-done | bytes 32800 | tf_op jit(solution)/shard_map/ppermute | solution.py:17
  19.4 0.9 select_maximum_fusion.4
  20.3 0.8 add_rsqrt_fusion
  21.1 0.1 broadcast_multiply_fusion
  21.3 1.0 fusion.74
  22.3 1.3 collective-permute-start.2
  23.6 5.0 %collective-permute-start.3 = (f32[32,1,32,128]{3,2,1,0:T(8,128)}, f32[32,1,32,128]{3,2,1,0:T(8,128)S(1)}, u32[]{:S(2)}, u32[]{:S(2)}) collective-permute-start(f32[32,1,32,128]{3,2,1,0:T(8,128)} %get-tuple-element.24), channel_id=1, source_target_pairs={{0,4},{4,8},{8,12},{12,16},{16,20},{20,24},{24,28},{1,5},{5,9},{9,... | collective-permute-start | bytes 1572872 | tf_op jit(solution)/shard_map/ppermute | solution.py:16
  28.6 0.8 stack.35
  29.4 7.9 %collective-permute-done.2 = f32[32,1,32,128]{3,2,1,0:T(8,128)S(1)} collective-permute-done((f32[32,1,32,128]{3,2,1,0:T(8,128)}, f32[32,1,32,128]{3,2,1,0:T(8,128)S(1)}, u32[]{:S(2)}, u32[]{:S(2)}) %collective-permute-start.2) | collective-permute-done | bytes 524320 | tf_op jit(solution)/shard_map/ppermute | solution.py:17
  37.3 11.5 %collective-permute-done.3 = f32[32,1,32,128]{3,2,1,0:T(8,128)S(1)} collective-permute-done((f32[32,1,32,128]{3,2,1,0:T(8,128)}, f32[32,1,32,128]{3,2,1,0:T(8,128)S(1)}, u32[]{:S(2)}, u32[]{:S(2)}) %collective-permute-start.3) | collective-permute-done | bytes 524320 | tf_op jit(solution)/shard_map/ppermute | solution.py:16
  48.8 2.2 %select_maximum_fusion = f32[32,4,34,130]{3,2,1,0:T(8,128)S(1)} fusion(f32[32,1,32,128]{3,2,1,0:T(8,128)S(1)} %collective-permute-done.2, f32[32,2,32,128]{3,2,1,0:T(8,128)S(1)} %broadcast_multiply_fusion, f32[32,1,32,128]{3,2,1,0:T(8,128)S(1)} %collective-permute-done.3), kind=kLoop, calls=%fused_computation.4 | loop fusion | flops 8486400 | bytes 4360192 | tf_op jit(solution)/shard_map/concatenate | solution.py:18
  51.1 2.3 %fusion.17 = f32[32,2,32,128]{3,2,1,0:T(8,128)S(1)} fusion(f32[32,2,32,128]{3,2,1,0:T(8,128)S(1)} %get-tuple-element.30, f32[32,4,34,130]{3,2,1,0:T(8,128)S(1)} %select_maximum_fusion, f32[32,2,32,128]{3,2,1,0:T(8,128)S(1)} %broadcast_multiply_fusion, f32[32,1,32,128]{3,2,1,0:T(8,128)} %copy-done.4, f32[32,1,32,128]{3,2,1,0:T(8,128)} %copy-done.3, ...), kind=kLoop, calls=%fused_computation.29 | loop fusion | flops 3932160 | bytes 8617984 | tf_op jit(solution)/shard_map/sub | solution.py:47
  53.5 0.2 multiply_reduce_fusion
  53.7 19.7 %all-reduce.4 = (f32[16]{0:T(128)S(1)}, f32[16]{0:T(128)S(1)}) all-reduce(f32[16]{0:T(128)S(1)} %get-tuple-element.6, f32[16]{0:T(128)S(1)} %get-tuple-element.5), channel_id=1, replica_groups=mesh['tile'=8,'vec'=4] {'tile'}, use_global_device_ids=true, to_apply=%region_1.2 | all-reduce | flops 32 | bytes 256 | tf_op jit(solution)/shard_map/psum | solution.py:79
  73.4 1.5 broadcast_multiply_fusion.1
  74.9 0.8 fusion.75
  75.7 1.3 collective-permute-start.4
  77.0 4.6 %collective-permute-start.5 = (f32[16,1,32,128]{3,2,1,0:T(8,128)}, f32[16,1,32,128]{3,2,1,0:T(8,128)S(1)}, u32[]{:S(2)}, u32[]{:S(2)}) collective-permute-start(f32[16,1,32,128]{3,2,1,0:T(8,128)} %get-tuple-element.27), channel_id=1, source_target_pairs={{0,4},{4,8},{8,12},{12,16},{16,20},{20,24},{24,28},{1,5},{5,9},{9,... | collective-permute-start | bytes 786440 | tf_op jit(solution)/shard_map/ppermute | solution.py:16
  81.6 0.8 stack.31
  82.4 1.0 constant_dynamic-update-slice_fusion.4
  83.3 0.8 collective-permute-done.4
  84.2 2.5 %collective-permute-done.5 = f32[16,1,32,128]{3,2,1,0:T(8,128)S(1)} collective-permute-done((f32[16,1,32,128]{3,2,1,0:T(8,128)}, f32[16,1,32,128]{3,2,1,0:T(8,128)S(1)}, u32[]{:S(2)}, u32[]{:S(2)}) %collective-permute-start.5) | collective-permute-done | bytes 262176 | tf_op jit(solution)/shard_map/ppermute | solution.py:16
  86.6 0.7 select_maximum_fusion.2
  87.4 2.4 %fusion.71 = (bf16[16,2,32,128]{3,2,1,0:T(8,128)(2,1)}, f32[16,2,32,128]{3,2,1,0:T(8,128)}, bf16[16,2,32,128]{3,2,1,0:T(8,128)(2,1)}) fusion(f32[16,2,32,128]{3,2,1,0:T(8,128)S(1)} %get-tuple-element.14, f32[16,4,34,130]{3,2,1,0:T(8,128)S(1)} %select_maximum_fusion.2, f32[2,32,128]{2,1,0:T(8,128)} %get-tuple-element.21, ...), kind=kLoop, calls=%fused_computation.137 | loop fusion | flops 2228224 | bytes 4947968 | tf_op jit(solution)/shard_map/convert.5
  89.8 1.1 stack.34
  90.9 1.0 constant_dynamic-update-slice_fusion.2
  91.9 0.9 copy-done.5
  92.8 0.0 all-reduce.7.cloned.1.call-start
  92.9 0.1 fusion.73
  93.0 0.1 stack.37
  93.1 0.8 stack.39
  93.9 0.8 stack.38
  94.7 25.8 %all-gather.2.cloned.1.call-done = bf16[3,64,8192]{2,1,0:T(8,128)(2,1)} async-done(((bf16[3,16,8192]{2,1,0:T(8,128)(2,1)}), bf16[3,64,8192]{2,1,0:T(8,128)(2,1)}) %all-gather.2.cloned.1.call-update) | async-done | bytes 3145744 | tf_op jit(solution)/shard_map/all_gather | solution.py:87
  120.6 4.2 %fusion.5 = f32[3,16,3,64]{3,1,2,0:T(8,128)} fusion(bf16[3,64,8192]{2,1,0:T(8,128)(2,1)} %all-gather.2.cloned.1.call-done, bf16[3,16,8192]{2,1,0:T(8,128)(2,1)} %copy-done.5), kind=kOutput, calls=%fused_computation.15 | convolution fusion | flops 150994944 | bytes 3969024 | tf_op jit(solution)/shard_map/aiv,bjv->aibj/dot_general | solution.py:88
  124.8 2.0 fusion.3
  126.8 0.6 convolution_bitcast_fusion
  127.4 0.1 copy-done.13
  127.5 0.5 fusion.12
  128.0 0.9 copy.18
  128.9 0.9 copy.17
  129.8 67.1 %all-reduce.7.cloned.1.call-done = (f32[3,16,3,64]{3,1,2,0:T(8,128)}, f32[3,16,3,64]{3,1,2,0:T(8,128)}) async-done(((f32[3,16,3,64]{3,1,2,0:T(8,128)}, f32[3,16,3,64]{3,1,2,0:T(8,128)}), (f32[3,16,3,64]{3,1,2,0:T(8,128)}, f32[3,16,3,64]{3,1,2,0:T(8,128)})) %all-reduce.7.cloned.1.call-update) | async-done | bytes 73744 | tf_op jit(solution)/shard_map/psum | solution.py:90
  196.9 1.6 broadcast_multiply_fusion.2
  (34 shorter events, 0.2 us)
Async XLA Ops:
  7.2 119.6 %copy-start = (bf16[3,64,64]{2,1,0:T(8,128)(2,1)S(1)}, bf16[3,64,64]{2,1,0:T(8,128)(2,1)}, u32[]{:S(2)}) copy-start(bf16[3,64,64]{2,1,0:T(8,128)(2,1)} %param.10) | copy-start | bytes 73732
  7.2 113.4 %all-gather.2.cloned.1.call-start = ((), (), s32[]{:S(2)}) async-start(), calls=%async_computation | async-start | bytes 3932160 | tf_op jit(solution)/shard_map/all_gather | solution.py:87
  8.7 8.6 %collective-permute-start = (f32[2,1,32,128]{3,2,1,0:T(8,128)S(1)}, f32[2,1,32,128]{3,2,1,0:T(8,128)S(1)}, u32[]{:S(2)}, u32[]{:S(2)}) collective-permute-start(f32[2,1,32,128]{3,2,1,0:T(8,128)S(1)} %get-tuple-element.34), channel_id=1, source_target_pairs={{0,4},{4,8},{8,12},{12,16},{16,20},{20,24},{24,28},{1,5},{5,9},{9,... | collective-permute-start | bytes 98312 | tf_op jit(solution)/shard_map/ppermute | solution.py:16
  13.6 5.8 %collective-permute-start.1 = (f32[2,1,32,128]{3,2,1,0:T(8,128)S(1)}, f32[2,1,32,128]{3,2,1,0:T(8,128)S(1)}, u32[]{:S(2)}, u32[]{:S(2)}) collective-permute-start(f32[2,1,32,128]{3,2,1,0:T(8,128)S(1)} %get-tuple-element.35), channel_id=1, source_target_pairs={{4,0},{8,4},{12,8},{16,12},{20,16},{24,20},{28,24},{5,1},{9,5},{13... | collective-permute-start | bytes 98312 | tf_op jit(solution)/shard_map/ppermute | solution.py:17
  22.3 15.0 %collective-permute-start.2 = (f32[32,1,32,128]{3,2,1,0:T(8,128)}, f32[32,1,32,128]{3,2,1,0:T(8,128)S(1)}, u32[]{:S(2)}, u32[]{:S(2)}) collective-permute-start(f32[32,1,32,128]{3,2,1,0:T(8,128)} %get-tuple-element.25), channel_id=1, source_target_pairs={{4,0},{8,4},{12,8},{16,12},{20,16},{24,20},{28,24},{5,1},{9,5},{13... | collective-permute-start | bytes 1572872 | tf_op jit(solution)/shard_map/ppermute | solution.py:17
  23.6 25.2 %collective-permute-start.3 = (f32[32,1,32,128]{3,2,1,0:T(8,128)}, f32[32,1,32,128]{3,2,1,0:T(8,128)S(1)}, u32[]{:S(2)}, u32[]{:S(2)}) collective-permute-start(f32[32,1,32,128]{3,2,1,0:T(8,128)} %get-tuple-element.24), channel_id=1, source_target_pairs={{0,4},{4,8},{8,12},{12,16},{16,20},{20,24},{24,28},{1,5},{5,9},{9,... | collective-permute-start | bytes 1572872 | tf_op jit(solution)/shard_map/ppermute | solution.py:16
  29.4 21.6 %copy-start.7 = (f32[2,32,128]{2,1,0:T(8,128)S(1)}, f32[2,32,128]{2,1,0:T(8,128)}, u32[]{:S(2)}) copy-start(f32[2,32,128]{2,1,0:T(8,128)} %get-tuple-element.18) | copy-start | bytes 98308
  29.4 21.6 %copy-start.8 = (f32[2,32,128]{2,1,0:T(8,128)S(1)}, f32[2,32,128]{2,1,0:T(8,128)}, u32[]{:S(2)}) copy-start(f32[2,32,128]{2,1,0:T(8,128)} %get-tuple-element.19) | copy-start | bytes 98308
  29.4 21.6 %copy-start.9 = (f32[2,32,128]{2,1,0:T(8,128)S(1)}, f32[2,32,128]{2,1,0:T(8,128)}, u32[]{:S(2)}) copy-start(f32[2,32,128]{2,1,0:T(8,128)} %get-tuple-element.20) | copy-start | bytes 98308
  29.4 21.7 %copy-start.10 = (f32[2,32,128]{2,1,0:T(8,128)S(1)}, f32[2,32,128]{2,1,0:T(8,128)}, u32[]{:S(2)}) copy-start(f32[2,32,128]{2,1,0:T(8,128)} %get-tuple-element.21) | copy-start | bytes 98308
  37.3 13.7 %copy-start.3 = (f32[32,1,32,128]{3,2,1,0:T(8,128)}, f32[32,1,32,128]{3,2,1,0:T(8,128)S(1)}, u32[]{:S(2)}) copy-start(f32[32,1,32,128]{3,2,1,0:T(8,128)S(1)} %collective-permute-done.2) | copy-start | bytes 1572868
  48.8 2.2 %copy-start.4 = (f32[32,1,32,128]{3,2,1,0:T(8,128)}, f32[32,1,32,128]{3,2,1,0:T(8,128)S(1)}, u32[]{:S(2)}) copy-start(f32[32,1,32,128]{3,2,1,0:T(8,128)S(1)} %collective-permute-done.3) | copy-start | bytes 1572868
  51.1 2.4 %copy-start.2 = (f32[16,2,32,128]{3,2,1,0:T(8,128)S(1)}, f32[16,2,32,128]{3,2,1,0:T(8,128)}, u32[]{:S(2)}) copy-start(f32[16,2,32,128]{3,2,1,0:T(8,128)} %param.6) | copy-start | bytes 1572868
  75.7 8.5 %collective-permute-start.4 = (f32[16,1,32,128]{3,2,1,0:T(8,128)}, f32[16,1,32,128]{3,2,1,0:T(8,128)S(1)}, u32[]{:S(2)}, u32[]{:S(2)}) collective-permute-start(f32[16,1,32,128]{3,2,1,0:T(8,128)} %get-tuple-element.28), channel_id=1, source_target_pairs={{4,0},{8,4},{12,8},{16,12},{20,16},{24,20},{28,24},{5,1},{9,5},{13... | collective-permute-start | bytes 786440 | tf_op jit(solution)/shard_map/ppermute | solution.py:17
  77.0 9.7 %collective-permute-start.5 = (f32[16,1,32,128]{3,2,1,0:T(8,128)}, f32[16,1,32,128]{3,2,1,0:T(8,128)S(1)}, u32[]{:S(2)}, u32[]{:S(2)}) collective-permute-start(f32[16,1,32,128]{3,2,1,0:T(8,128)} %get-tuple-element.27), channel_id=1, source_target_pairs={{0,4},{4,8},{8,12},{12,16},{16,20},{20,24},{24,28},{1,5},{5,9},{9,... | collective-permute-start | bytes 786440 | tf_op jit(solution)/shard_map/ppermute | solution.py:16
  89.8 4.1 %copy-start.6 = (bf16[16,2,32,128]{3,2,1,0:T(8,128)(2,1)S(1)}, bf16[16,2,32,128]{3,2,1,0:T(8,128)(2,1)}, u32[]{:S(2)}) copy-start(bf16[16,2,32,128]{3,2,1,0:T(8,128)(2,1)} %get-tuple-element.11) | copy-start | bytes 786436
  91.9 0.9 copy-start.5
  92.8 104.1 %all-reduce.7.cloned.1.call-start = ((), (), s32[]{:S(2)}) async-start(), calls=%async_computation.1 | async-start | bytes 294912 | tf_op jit(solution)/shard_map/psum | solution.py:90
  120.6 4.2 %copy-start.1 = (bf16[3,64,8192]{2,1,0:T(8,128)(2,1)S(1)}, bf16[3,64,8192]{2,1,0:T(8,128)(2,1)}, u32[]{:S(2)}) copy-start(bf16[3,64,8192]{2,1,0:T(8,128)(2,1)} %all-gather.2.cloned.1.call-done) | copy-start | bytes 9437188
  120.6 4.2 %copy-start.11 = (bf16[1,16,8192]{2,1,0:T(8,128)(2,1)S(1)}, bf16[1,16,8192]{2,1,0:T(8,128)(2,1)}, u32[]{:S(2)}) copy-start(bf16[1,16,8192]{2,1,0:T(8,128)(2,1)} %stack.39) | copy-start | bytes 786436
  120.6 4.2 %copy-start.12 = (bf16[1,16,8192]{2,1,0:T(8,128)(2,1)S(1)}, bf16[1,16,8192]{2,1,0:T(8,128)(2,1)}, u32[]{:S(2)}) copy-start(bf16[1,16,8192]{2,1,0:T(8,128)(2,1)} %stack.38) | copy-start | bytes 786436
  126.8 0.8 copy-start.13
Sparse Core Ops, SparseCore 0:
  92.9 27.5 all-gather.1
  126.9 69.9 all-reduce.6
where the time goes:
time: 206 us; the launch traced here: 205 us
  waiting for transfers between devices  118 us (57%)
  blocking collectives  19.7 us (10%)
  starting transfers between devices  18.3 us (9%)
  between operations  15 us (7%)
  other arithmetic  14.9 us (7%)
  local copies, waits for them, and re-layouts  12.4 us (6%)
  matrix products  7.3 us (4%)
    psum x1, waiting for transfers between devices, shards(): gram_s, gram_a = lax.psum((gram_s, gram_a), 'tile')  67.1 us
    all_gather x1, waiting for transfers between devices, shards(): whole = lax.all_gather(basis, 'vec', axis=1, tiled=True)  25.8 us
    psum x1, blocking collectives, shards(): num, den = lax.psum((num, den), 'tile')  19.7 us
    ppermute x3, starting transfers between devices, with_halo(): before = lax.ppermute(last, axis, up)  14.4 us
    ppermute x3, waiting for transfers between devices, with_halo(): before = lax.ppermute(last, axis, up)  14 us
    ppermute x3, waiting for transfers between devices, with_halo(): after = lax.ppermute(first, axis, down)  10.8 us
    unnamed x33, local copies, waits for them, and re-layouts  4.89 us
    dot_general x1, matrix products, shards(): jnp.einsum('aiv,bjv->aibj', basis, whole, preferred_element_type=jnp.floa...  4.22 us
  transfers between devices with their start and end apart: 8, of which 7 were waited for; matrix products, arithmetic and copies ran while one was open for 5% of the time, Pallas kernels for 0%

commit v1 on v0

v1 whole, which is shorter than its diff:
```python
import functools

import jax
import jax.numpy as jnp
from jax import lax
from jax.experimental import pallas as pl
from jax.experimental.pallas import tpu as pltpu
from jax.sharding import PartitionSpec as P

MESH = pl.DeviceIdType.MESH
F32 = jnp.float32
BF16 = jnp.bfloat16
Q = 6
CH = 1024


def kernel(
    T, nc, cy, cz, nvox,
    x_ref, p_ref, int_ref, cnt_ref, cfx_ref, cfp_ref,
    xo_ref, po_ref, ar_ref, g_ref,
    igb, igh, hb, hh, coef, W, L, axf, rf, lbuf, lamb,
    gpart, grs, gout,
    ig_s, ig_r, h_s, h_r, w_s, w_r, lam_s, lam_r, rs_s, rs_r, ag_s, ag_r,
):
    t = lax.axis_index("tile")
    v = lax.axis_index("vec")
    sib = v + 1 - 2 * (v % 2)
    across = (v + 2) % 4
    diag = (sib + 2) % 4
    tl = (t + T - 1) % T
    tr = (t + 1) % T
    rows = 2 * cy
    nl = rows * cz

    def rc(src, dst, ss, rs, tile, vec):
        return pltpu.make_async_remote_copy(
            src_ref=src, dst_ref=dst, send_sem=ss, recv_sem=rs,
            device_id={"tile": tile, "vec": vec}, device_id_type=MESH)

    barrier = pltpu.get_barrier_semaphore()
    for d in range(1, T):
        pl.semaphore_signal(barrier, inc=1, device_id={"tile": (t + d) % T, "vec": v}, device_id_type=MESH)
    pl.semaphore_signal(barrier, inc=1, device_id={"tile": t, "vec": sib}, device_id_type=MESH)
    pl.semaphore_signal(barrier, inc=1, device_id={"tile": t, "vec": across}, device_id_type=MESH)

    yy = lax.broadcasted_iota(jnp.int32, (cy, cz), 0)
    zz = lax.broadcasted_iota(jnp.int32, (cy, cz), 1)
    cnt = cnt_ref[0]
    for p in range(2):
        fg = jnp.where((p * cy + yy) * cz + zz < cnt, 1.0, 0.0).astype(F32)
        igb[p, 0] = int_ref[p]
        igb[p, 1] = fg * 0.9 + 0.1

    def to_halo(f, src):
        @pl.loop(0, nc)
        def _(c):
            for p in range(2):
                hb[f, p, c] = src[pl.ds(c * rows + p * cy, cy), :].astype(BF16)

    def spread(src, dsts):
        for r in range(rows):
            val = src[pl.ds(r, nc, stride=rows), :].astype(BF16)
            for dst in dsts:
                dst[:, r * cz:(r + 1) * cz] = val

    to_halo(0, x_ref)
    spread(x_ref, (W.at[0, v], L.at[0]))
    spread(p_ref, (W.at[1, v], L.at[2]))
    to_halo(1, p_ref)

    @pl.when(t == 0)
    def _():
        hh[0, 0] = jnp.zeros((nc, cy, cz), BF16)
        hh[1, 0] = jnp.zeros((nc, cy, cz), BF16)
        hh[2, 0] = jnp.zeros((nc, cy, cz), BF16)
        igh[0] = jnp.zeros((2, 2, cy, cz), F32)

    @pl.when(t == T - 1)
    def _():
        hh[0, 1] = jnp.zeros((nc, cy, cz), BF16)
        hh[1, 1] = jnp.zeros((nc, cy, cz), BF16)
        hh[2, 1] = jnp.zeros((nc, cy, cz), BF16)
        igh[1] = jnp.zeros((2, 2, cy, cz), F32)

    pl.semaphore_wait(barrier, T + 1)

    def ig_left():
        return rc(igb, igh.at[1], ig_s.at[0], ig_r.at[1], tl, v)

    def ig_right():
        return rc(igb, igh.at[0], ig_s.at[1], ig_r.at[0], tr, v)

    def h_left(f):
        return rc(hb.at[f, 0], hh.at[f, 1], h_s.at[f, 0], h_r.at[f, 1], tl, v)

    def h_right(f):
        return rc(hb.at[f, 1], hh.at[f, 0], h_s.at[f, 1], h_r.at[f, 0], tr, v)

    def both(left, right, what):
        @pl.when(t > 0)
        def _():
            c = right() if what == "wait_recv" else left()
            getattr(c, what)()

        @pl.when(t < T - 1)
        def _():
            c = left() if what == "wait_recv" else right()
            getattr(c, what)()

    def halo(f, what):
        both(lambda: h_left(f), lambda: h_right(f), what)

    def to_sib(f):
        return rc(W.at[f, v], W.at[f, v], w_s.at[f, 0], w_r.at[f, 0], t, sib)

    def to_across(f):
        return rc(W.at[f, v], W.at[f, v], w_s.at[f, 1], w_r.at[f, 1], t, across)

    def relay(f):
        return rc(W.at[f, across], W.at[f, across], w_s.at[f, 2], w_r.at[f, 2], t, sib)

    both(ig_left, ig_right, "start")
    halo(0, "start")
    to_across(0).start()
    to_across(1).start()
    to_sib(0).start()
    to_sib(1).start()
    halo(1, "start")

    pick = jnp.where(
        lax.broadcasted_iota(jnp.int32, (nc, 4 * nc), 1) == v * nc + lax.broadcasted_iota(jnp.int32, (nc, 4 * nc), 0),
        1.0, 0.0).astype(BF16)

    def own_t(m):
        return lax.dot_general(pick, m, (((1,), (1,)), ((), ())), preferred_element_type=F32)

    zero = jnp.zeros((nc, 4 * nc), F32)
    ct_x = jnp.concatenate([own_t(cfx_ref[0]), zero], axis=0).astype(BF16)
    ct_r = jnp.concatenate([own_t(cfx_ref[1]), own_t(cfp_ref[0])], axis=0).astype(BF16)
    ct_p = jnp.concatenate([own_t(cfx_ref[2]), own_t(cfp_ref[1])], axis=0).astype(BF16)

    both(ig_left, ig_right, "wait_recv")
    im = [igh[0, 0, 0], igh[0, 1, 0], igb[0, 0], igb[1, 0], igh[1, 0, 0], igh[1, 1, 0]]
    gg = [igh[0, 0, 1], igh[0, 1, 1], igb[0, 1], igb[1, 1], igh[1, 0, 1], igh[1, 1, 1]]

    def up(a, axis):
        return pltpu.roll(a, a.shape[axis] - 1, axis)

    def down(a, axis):
        return pltpu.roll(a, 1, axis)

    wx = [jnp.exp(-((im[k] - im[k + 1]) ** 2)) * gg[k] * gg[k + 1] for k in range(5)]
    wx[1] = jnp.where(t > 0, wx[1], 0.0)
    wx[3] = jnp.where(t < T - 1, wx[3], 0.0)
    wx[0] = jnp.where(t > 0, wx[0], 0.0)
    wx[4] = jnp.where(t < T - 1, wx[4], 0.0)
    inv, wys, wzs = {}, {}, {}
    for k in range(1, 5):
        wy = jnp.where(yy < cy - 1, jnp.exp(-((im[k] - up(im[k], 0)) ** 2)) * gg[k] * up(gg[k], 0), 0.0)
        wz = jnp.where(zz < cz - 1, jnp.exp(-((im[k] - up(im[k], 1)) ** 2)) * gg[k] * up(gg[k], 1), 0.0)
        deg = wx[k] + wx[k - 1] + wy + down(wy, 0) + wz + down(wz, 1)
        inv[k] = lax.rsqrt(deg)
        wys[k], wzs[k] = wy, wz
    cm = jnp.where(t > 0, inv[1] * wx[1] * inv[2], 0.0)
    c0 = inv[2] * wx[2] * inv[3]
    cp = jnp.where(t < T - 1, inv[3] * wx[3] * inv[4], 0.0)
    coef[0, 0] = cm
    coef[0, 1] = c0
    coef[0, 2] = cp
    for p in range(2):
        k = p + 2
        cyu = inv[k] * wys[k] * up(inv[k], 0)
        czu = inv[k] * wzs[k] * up(inv[k], 1)
        coef[1, p] = cyu
        coef[2, p] = down(cyu, 0)
        coef[3, p] = czu
        coef[4, p] = down(czu, 1)

    def stencil(src, c, f):
        fs = [src[pl.ds(c * rows, cy), :], src[pl.ds(c * rows + cy, cy), :]]
        out = []
        for p in range(2):
            a = fs[p]
            s = coef[1, p] * up(a, 0) + coef[2, p] * down(a, 0)
            s = s + coef[3, p] * up(a, 1) + coef[4, p] * down(a, 1)
            s = s + coef[0, 1] * fs[1 - p]
            s = s + coef[0, 2 * p] * hh[f, p, c].astype(F32)
            out.append(a - s)
        return fs, out

    halo(0, "wait_recv")
    lbuf[...] = jnp.zeros_like(lbuf)

    @pl.loop(0, nc)
    def _(c):
        fs, out = stencil(x_ref, c, 0)
        axf[pl.ds(c * rows, cy), :] = out[0]
        axf[pl.ds(c * rows + cy, cy), :] = out[1]
        num = fs[0] * out[0] + fs[1] * out[1]
        den = fs[0] * fs[0] + fs[1] * fs[1]
        lbuf[pl.ds(c, 1), :] = jnp.sum(num, axis=0, keepdims=True)
        lbuf[pl.ds(nc + c, 1), :] = jnp.sum(den, axis=0, keepdims=True)

    lamb[0] = lax.dot_general(
        jnp.ones((8, cz), F32), lbuf[...], (((1,), (1,)), ((), ())),
        precision=lax.Precision.HIGHEST, preferred_element_type=F32)

    def lam_copy(d):
        return rc(lamb.at[0], lamb.at[d], lam_s.at[d], lam_r.at[d], (t + d) % T, v)

    for d in range(1, T):
        lam_copy(d).start()
    spread(axf, (L.at[3],))
    for d in range(1, T):
        lam_copy(d).wait_recv()
    tot = lamb[0]
    for d in range(1, T):
        tot = tot + lamb[d]

    for c in range(nc):
        lam = tot[0:1, c:c + 1] / tot[0:1, nc + c:nc + c + 1]
        rr = axf[pl.ds(c * rows, rows), :] - lam * x_ref[pl.ds(c * rows, rows), :]
        rf[pl.ds(c * rows, rows), :] = rr
        hb[2, 0, c] = rr[:cy].astype(BF16)
        hb[2, 1, c] = rr[cy:].astype(BF16)
    halo(2, "start")
    spread(rf, (W.at[2, v], L.at[1]))
    to_across(2).start()
    to_sib(2).start()

    halo(1, "wait_recv")

    @pl.loop(0, nc)
    def _(c):
        _, out = stencil(p_ref, c, 1)
        axf[pl.ds(c * rows, cy), :] = out[0]
        axf[pl.ds(c * rows + cy, cy), :] = out[1]

    spread(axf, (L.at[5],))
    to_across(0).wait_recv()
    relay(0).start()
    to_across(1).wait_recv()
    relay(1).start()

    halo(2, "wait_recv")

    @pl.loop(0, nc)
    def _(c):
        _, out = stencil(rf, c, 2)
        ar_ref[pl.ds(c * rows, cy), :] = out[0]
        ar_ref[pl.ds(c * rows + cy, cy), :] = out[1]

    spread(ar_ref, (L.at[4],))

    def gram(lo, hi):
        def body(k, acc):
            ch = pl.ds(pl.multiple_of(k * CH, CH), CH)
            a = L[:, :, ch].reshape(6 * nc, CH)
            b = W[lo:hi, :, :, ch].reshape((hi - lo) * 4 * nc, CH)
            return acc + lax.dot_general(a, b, (((1,), (1,)), ((), ())), preferred_element_type=F32)
        return lax.fori_loop(0, nl // CH, body, jnp.zeros((6 * nc, (hi - lo) * 4 * nc), F32))

    def rs_copy(e, d):
        dst = (t + d) % T
        return rc(gpart.at[e, dst], grs.at[e, d], rs_s.at[e, d], rs_r.at[e, d], dst, v)

    def rs_each(e, what):
        for d in range(1, T):
            @pl.when((t + d) % T < Q)
            def _():
                getattr(rs_copy(e, d), what)()

    def ag_copy(e, d, q):
        return rc(gout.at[e, q], gout.at[e, q], ag_s.at[e, d], ag_r.at[e, q], (t + d) % T, v)

    def reduce(e):
        @pl.when(t < Q)
        def _():
            total = gpart[e, t]
            for d in range(1, T):
                rc(gpart.at[e, 0], grs.at[e, d], rs_s.at[e, d], rs_r.at[e, d], (t + d) % T, v).wait_recv()
                total = total + grs[e, d]
            gout[e, t] = total * (1.0 / nvox)
            for d in range(1, T):
                ag_copy(e, d, t).start()

    to_sib(0).wait_recv()
    to_sib(1).wait_recv()
    relay(0).wait_recv()
    relay(1).wait_recv()
    gx = gram(0, 2)
    for q in range(Q):
        gpart[0, q] = gx[q * nc:(q + 1) * nc, :]
    rs_each(0, "start")

    to_across(2).wait_recv()
    relay(2).start()
    to_sib(2).wait_recv()
    reduce(0)
    relay(2).wait_recv()
    gr = gram(2, 3)
    pad = jnp.zeros((nc, 4 * nc), F32)
    for q in range(Q):
        gpart[1, q] = jnp.concatenate([gr[q * nc:(q + 1) * nc, :], pad], axis=1)
    rs_each(1, "start")

    ct = jnp.concatenate([ct_x, ct_p, ct_r], axis=1)

    @pl.loop(0, nl // CH)
    def _(k):
        ch = pl.ds(pl.multiple_of(k * CH, CH), CH)
        o = jnp.dot(ct, W[:, :, :, ch].reshape(12 * nc, CH), preferred_element_type=F32)
        for r in range(CH // cz):
            at = pl.ds(k * (CH // cz) + r, nc, stride=rows)
            xo_ref[at, :] = o[:nc, r * cz:(r + 1) * cz]
            po_ref[at, :] = o[nc:, r * cz:(r + 1) * cz]

    reduce(1)
    for e in range(2):
        for q in range(Q):
            @pl.when(t != q)
            def _():
                ag_copy(e, 1, q).wait_recv()
    n4 = 4 * nc
    for h in range(2):
        for a in range(3):
            q = 3 * h + a
            xp = gout[0, q]
            g_ref[h, a * nc:(a + 1) * nc, :] = jnp.concatenate(
                [xp[:, :n4], gout[1, q][:, :n4], xp[:, n4:]], axis=1)

    both(ig_left, ig_right, "wait_send")
    for f in range(3):
        halo(f, "wait_send")
        to_across(f).wait_send()
        to_sib(f).wait_send()
        relay(f).wait_send()
    for d in range(1, T):
        lam_copy(d).wait_send()
    for e in range(2):
        rs_each(e, "wait_send")

        @pl.when(t < Q)
        def _():
            for d in range(1, T):
                ag_copy(e, d, t).wait_send()


def shards(T, vectors, previous, intensity, counts, coef_x, coef_p):
    nc, cx, cy, cz = vectors.shape
    rows = cx * cy
    nl = rows * cz
    vm = pl.BlockSpec(memory_space=pltpu.VMEM)
    dma = pltpu.SemaphoreType.DMA
    xo, po, ar, g = pl.pallas_call(
        functools.partial(kernel, T, nc, cy, cz, nl * T),
        out_shape=[jax.ShapeDtypeStruct((nc * rows, cz), F32)] * 3 + [jax.ShapeDtypeStruct((2, 3 * nc, 12 * nc), F32)],
        in_specs=[vm, vm, vm, pl.BlockSpec(memory_space=pltpu.SMEM), vm, vm],
        out_specs=[vm] * 4,
        scratch_shapes=[
            pltpu.VMEM((2, 2, cy, cz), F32),
            pltpu.VMEM((2, 2, 2, cy, cz), F32),
            pltpu.VMEM((3, 2, nc, cy, cz), BF16),
            pltpu.VMEM((3, 2, nc, cy, cz), BF16),
            pltpu.VMEM((5, 3, cy, cz), F32),
            pltpu.VMEM((3, 4, nc, nl), BF16),
            pltpu.VMEM((6, nc, nl), BF16),
            pltpu.VMEM((nc * rows, cz), F32),
            pltpu.VMEM((nc * rows, cz), F32),
            pltpu.VMEM((128, cz), F32),
            pltpu.VMEM((T, 8, 128), F32),
            pltpu.VMEM((2, Q, nc, 8 * nc), F32),
            pltpu.VMEM((2, T, nc, 8 * nc), F32),
            pltpu.VMEM((2, Q, nc, 8 * nc), F32),
            dma((2,)), dma((2,)), dma((3, 2)), dma((3, 2)), dma((3, 3)), dma((3, 3)),
            dma((T,)), dma((T,)), dma((2, T)), dma((2, T)), dma((2, T)), dma((2, Q)),
        ],
        compiler_params=pltpu.CompilerParams(
            collective_id=0, has_side_effects=True, vmem_limit_bytes=40 * 1024 * 1024),
    )(vectors.reshape(nc * rows, cz), previous.reshape(nc * rows, cz), intensity, counts, coef_x, coef_p)
    shape = (nc, cx, cy, cz)
    return (
        xo.reshape(shape), po.reshape(shape), ar.reshape(shape),
        g[0].reshape(3, nc, 3, 4 * nc), g[1].reshape(3, nc, 3, 4 * nc),
    )


def solution(mesh):
    cols = P("vec", "tile", None, None)
    gram = P(None, "vec", None, None)
    return jax.shard_map(
        functools.partial(shards, mesh.shape["tile"]),
        mesh=mesh,
        in_specs=(cols, cols, P("tile", None, None), P("tile"), P(), P()),
        out_specs=(cols, cols, cols, gram, gram),
        check_vma=False,
    )
```

time: 206 us -> 58.4 us (0.28)
  waiting for transfers between devices: 118 us -> 0 us
  Pallas kernels: 0 us -> 48.5 us
  blocking collectives: 19.7 us -> 0 us
  starting transfers between devices: 18.3 us -> 0 us
  other arithmetic: 14.9 us -> 0 us
  between operations: 15 us -> 1.32 us
  matrix products: 7.3 us -> 0 us
  local copies, waits for them, and re-layouts: 12.4 us -> 8.23 us
    psum x1 -> x0, waiting for transfers between devices: 67.1 us -> none  [shards(): gram_s, gram_a = lax.psum((gram_s, gram_a), 'tile')]
    pallas_call x0 -> x1, Pallas kernels: none -> 48.5 us  [shards(): pl.pallas_call(functools.partial(kernel, T, nc, cy, cz, nl * T), out_shap...]
    all_gather x1 -> x0, waiting for transfers between devices: 25.8 us -> none  [shards(): whole = lax.all_gather(basis, 'vec', axis=1, tiled=True)]
    ppermute x6 -> x0, waiting for transfers between devices: 24.8 us -> none  [the longest x3 14 us: with_halo(): before = lax.ppermute(last, axis, up)]
    psum x1 -> x0, blocking collectives: 19.7 us -> none  [shards(): num, den = lax.psum((num, den), 'tile')]
    ppermute x6 -> x0, starting transfers between devices: 18.3 us -> none  [the longest x3 14.4 us: with_halo(): before = lax.ppermute(last, axis, up)]
    dot_general x4 -> x0, matrix products: 7.3 us -> none  [the longest x1 4.22 us: shards(): jnp.einsum('aiv,bjv->aibj', basis, whole, preferred_element_type=jnp.floa...]
    another operation x7 -> x2, local copies, waits for them, and re-layouts: 5.47 us -> 0.18 us  [the longest x1 0.09 us: shards(): g[0].reshape(3, nc, 3, 4 * nc)]
  transfers between devices with their start and end apart: 8 -> 0, of which waited for: 7 -> 0; matrix products, arithmetic and copies ran while one was open for 5% -> 0% of each run, Pallas kernels for 0% -> 0%
where the time goes in v1:
time: 58.4 us; the launch traced here: 58 us
  Pallas kernels  48.5 us (83%)
  local copies, waits for them, and re-layouts  8.23 us (14%)
  between operations  1.32 us (2%)
    pallas_call x1, Pallas kernels, shards(): pl.pallas_call(functools.partial(kernel, T, nc, cy, cz, nl * T), out_shap...  48.5 us
    unnamed x15, local copies, waits for them, and re-layouts  8.04 us

profile of v1, /device:TPU:0, one launch (start us, length us, event | category | flops | bytes accessed | tf_op | source)
XLA Modules:
  0.0 58.0 jit_solution(1003355573289672642)
XLA Ops:
  1.3 0.0 copy-start
  1.3 1.0 %copy-done = f32[16,2,32,128]{3,2,1,0:T(8,128)S(1)} copy-done((f32[16,2,32,128]{3,2,1,0:T(8,128)S(1)}, f32[16,2,32,128]{3,2,1,0:T(8,128)}, u32[]{:S(2)}) %copy-start) | copy-done | bytes 524312
  2.3 0.0 copy-start.1
  2.3 1.0 %copy-done.1 = f32[16,2,32,128]{3,2,1,0:T(8,128)S(1)} copy-done((f32[16,2,32,128]{3,2,1,0:T(8,128)S(1)}, f32[16,2,32,128]{3,2,1,0:T(8,128)}, u32[]{:S(2)}) %copy-start.1) | copy-done | bytes 524312
  3.4 0.0 copy-start.2
  3.4 0.8 %copy-done.2 = bf16[3,64,64]{2,1,0:T(8,128)(2,1)S(1)} copy-done((bf16[3,64,64]{2,1,0:T(8,128)(2,1)S(1)}, bf16[3,64,64]{2,1,0:T(8,128)(2,1)}, u32[]{:S(2)}) %copy-start.2) | copy-done | bytes 24600
  4.2 0.0 copy-start.3
  4.2 0.8 %copy-done.3 = f32[2,32,128]{2,1,0:T(8,128)S(1)} copy-done((f32[2,32,128]{2,1,0:T(8,128)S(1)}, f32[2,32,128]{2,1,0:T(8,128)}, u32[]{:S(2)}) %copy-start.3) | copy-done | bytes 32792
  4.9 0.0 copy-start.4
  4.9 0.8 %copy-done.4 = bf16[2,64,64]{2,1,0:T(8,128)(2,1)S(1)} copy-done((bf16[2,64,64]{2,1,0:T(8,128)(2,1)S(1)}, bf16[2,64,64]{2,1,0:T(8,128)(2,1)}, u32[]{:S(2)}) %copy-start.4) | copy-done | bytes 16408
  5.7 48.5 %shard_map.101 = (f32[1024,128]{1,0:T(8,128)S(1)}, f32[1024,128]{1,0:T(8,128)S(1)}, f32[1024,128]{1,0:T(8,128)S(1)}, f32[2,48,192]{2,1,0:T(8,128)S(1)}) custom-call(f32[1024,128]{1,0:T(8,128)S(1)} %bitcast.5, f32[1024,128]{1,0:T(8,128)S(1)} %bitcast.6, f32[2,32,128]{2,1,0:T(8,128)S(1)} %copy-done.3, s32[1]{0:T(128)S(6)} %copy.18.cnt_ref, ...), custom_call_target="tpu_custom_call" | custom-call | tf_op jit(solution)/shard_map/pallas_call | solution.py:355
  54.2 0.1 reshape_squeeze.6
  54.3 0.6 %copy.13 = f32[3,16,3,64]{3,1,2,0:T(8,128)} copy(f32[3,16,3,64]{3,2,1,0:T(4,128)S(1)} %reshape_squeeze.6) | data formatting | bytes 73728
  54.9 0.1 reshape_squeeze.7
  55.0 0.6 %copy.14 = f32[3,16,3,64]{3,1,2,0:T(8,128)} copy(f32[3,16,3,64]{3,2,1,0:T(4,128)S(1)} %reshape_squeeze.7) | data formatting | bytes 73728
  55.6 0.8 %copy.19 = f32[16,2,32,128]{3,2,1,0:T(8,128)} copy(f32[16,2,32,128]{3,2,1,0:T(8,128)S(1)} %bitcast.9) | data formatting | bytes 1048576
  56.4 0.8 %copy.20 = f32[16,2,32,128]{3,2,1,0:T(8,128)} copy(f32[16,2,32,128]{3,2,1,0:T(8,128)S(1)} %bitcast.8) | data formatting | bytes 1048576
  57.2 0.8 %copy.21 = f32[16,2,32,128]{3,2,1,0:T(8,128)} copy(f32[16,2,32,128]{3,2,1,0:T(8,128)S(1)} %bitcast.7) | data formatting | bytes 1048576
  (1 shorter events, 0.0 us)
Async XLA Ops:
  1.3 1.0 %copy-start = (f32[16,2,32,128]{3,2,1,0:T(8,128)S(1)}, f32[16,2,32,128]{3,2,1,0:T(8,128)}, u32[]{:S(2)}) copy-start(f32[16,2,32,128]{3,2,1,0:T(8,128)} %param.6) | copy-start | bytes 1572868
  2.3 1.0 %copy-start.1 = (f32[16,2,32,128]{3,2,1,0:T(8,128)S(1)}, f32[16,2,32,128]{3,2,1,0:T(8,128)}, u32[]{:S(2)}) copy-start(f32[16,2,32,128]{3,2,1,0:T(8,128)} %param.7) | copy-start | bytes 1572868
  3.4 0.8 %copy-start.2 = (bf16[3,64,64]{2,1,0:T(8,128)(2,1)S(1)}, bf16[3,64,64]{2,1,0:T(8,128)(2,1)}, u32[]{:S(2)}) copy-start(bf16[3,64,64]{2,1,0:T(8,128)(2,1)} %cfx_ref.1) | copy-start | bytes 73732
  4.2 0.8 %copy-start.3 = (f32[2,32,128]{2,1,0:T(8,128)S(1)}, f32[2,32,128]{2,1,0:T(8,128)}, u32[]{:S(2)}) copy-start(f32[2,32,128]{2,1,0:T(8,128)} %int_ref.1) | copy-start | bytes 98308
  4.9 0.8 %copy-start.4 = (bf16[2,64,64]{2,1,0:T(8,128)(2,1)S(1)}, bf16[2,64,64]{2,1,0:T(8,128)(2,1)}, u32[]{:S(2)}) copy-start(bf16[2,64,64]{2,1,0:T(8,128)(2,1)} %cfp_ref.1) | copy-start | bytes 49156

commit v2 on v1

--- a/solution.py
+++ b/solution.py
@@ -16,9 +16,10 @@
 
 def kernel(
     T, nc, cy, cz, nvox,
-    x_ref, p_ref, int_ref, cnt_ref, cfx_ref, cfp_ref,
-    xo_ref, po_ref, ar_ref, g_ref,
-    igb, igh, hb, hh, coef, W, L, axf, rf, lbuf, lamb,
+    x_hbm, p_hbm, int_hbm, cnt_ref, cfx_hbm, cfp_hbm,
+    xo_ref, po_ref, ar_ref, gs_ref, ga_ref,
+    x_ref, p_ref, int_ref, cfx_ref, cfp_ref, in_s,
+    igb, igh, hb, hh, coef, W, L, axf, apf, rf, lbuf, lamb, lamr,
     gpart, grs, gout,
     ig_s, ig_r, h_s, h_r, w_s, w_r, lam_s, lam_r, rs_s, rs_r, ag_s, ag_r,
 ):
@@ -26,7 +27,6 @@
     v = lax.axis_index("vec")
     sib = v + 1 - 2 * (v % 2)
     across = (v + 2) % 4
-    diag = (sib + 2) % 4
     tl = (t + T - 1) % T
     tr = (t + 1) % T
     rows = 2 * cy
@@ -37,22 +37,31 @@
             src_ref=src, dst_ref=dst, send_sem=ss, recv_sem=rs,
             device_id={"tile": tile, "vec": vec}, device_id_type=MESH)
 
+    loads = [
+        pltpu.make_async_copy(a, b, in_s.at[k])
+        for k, (a, b) in enumerate((
+            (x_hbm, x_ref), (int_hbm, int_ref), (p_hbm, p_ref), (cfx_hbm, cfx_ref), (cfp_hbm, cfp_ref)))
+    ]
     barrier = pltpu.get_barrier_semaphore()
     for d in range(1, T):
         pl.semaphore_signal(barrier, inc=1, device_id={"tile": (t + d) % T, "vec": v}, device_id_type=MESH)
     pl.semaphore_signal(barrier, inc=1, device_id={"tile": t, "vec": sib}, device_id_type=MESH)
     pl.semaphore_signal(barrier, inc=1, device_id={"tile": t, "vec": across}, device_id_type=MESH)
 
+    for load in loads:
+        load.start()
+
     yy = lax.broadcasted_iota(jnp.int32, (cy, cz), 0)
     zz = lax.broadcasted_iota(jnp.int32, (cy, cz), 1)
     cnt = cnt_ref[0]
+    loads[1].wait()
     for p in range(2):
         fg = jnp.where((p * cy + yy) * cz + zz < cnt, 1.0, 0.0).astype(F32)
         igb[p, 0] = int_ref[p]
         igb[p, 1] = fg * 0.9 + 0.1
 
     def to_halo(f, src):
-        @pl.loop(0, nc)
+        @pl.loop(0, nc, unroll=4)
         def _(c):
             for p in range(2):
                 hb[f, p, c] = src[pl.ds(c * rows + p * cy, cy), :].astype(BF16)
@@ -63,10 +72,8 @@
             for dst in dsts:
                 dst[:, r * cz:(r + 1) * cz] = val
 
+    loads[0].wait()
     to_halo(0, x_ref)
-    spread(x_ref, (W.at[0, v], L.at[0]))
-    spread(p_ref, (W.at[1, v], L.at[2]))
-    to_halo(1, p_ref)
 
     @pl.when(t == 0)
     def _():
@@ -121,11 +128,16 @@
 
     both(ig_left, ig_right, "start")
     halo(0, "start")
+    loads[2].wait()
+    to_halo(1, p_ref)
+    spread(x_ref, (W.at[0, v], L.at[0]))
     to_across(0).start()
+    to_sib(0).start()
+    spread(p_ref, (W.at[1, v], L.at[2]))
     to_across(1).start()
-    to_sib(0).start()
     to_sib(1).start()
-    halo(1, "start")
+    loads[3].wait()
+    loads[4].wait()
 
     pick = jnp.where(
         lax.broadcasted_iota(jnp.int32, (nc, 4 * nc), 1) == v * nc + lax.broadcasted_iota(jnp.int32, (nc, 4 * nc), 0),
@@ -176,31 +188,44 @@
         coef[3, p] = czu
         coef[4, p] = down(czu, 1)
 
-    def stencil(src, c, f):
+    def inner(src, dst, c):
         fs = [src[pl.ds(c * rows, cy), :], src[pl.ds(c * rows + cy, cy), :]]
-        out = []
         for p in range(2):
             a = fs[p]
             s = coef[1, p] * up(a, 0) + coef[2, p] * down(a, 0)
             s = s + coef[3, p] * up(a, 1) + coef[4, p] * down(a, 1)
             s = s + coef[0, 1] * fs[1 - p]
-            s = s + coef[0, 2 * p] * hh[f, p, c].astype(F32)
-            out.append(a - s)
-        return fs, out
+            dst[pl.ds(c * rows + p * cy, cy), :] = a - s
+
+    def outer(f, p, c):
+        return coef[0, 2 * p] * hh[f, p, c].astype(F32)
+
+    @pl.loop(0, nc, unroll=4)
+    def _(c):
+        inner(x_ref, axf, c)
+
+    @pl.loop(0, nc, unroll=4)
+    def _(c):
+        inner(p_ref, apf, c)
+
+    lbuf[...] = jnp.zeros_like(lbuf)
 
     halo(0, "wait_recv")
-    lbuf[...] = jnp.zeros_like(lbuf)
-
-    @pl.loop(0, nc)
-    def _(c):
-        fs, out = stencil(x_ref, c, 0)
-        axf[pl.ds(c * rows, cy), :] = out[0]
-        axf[pl.ds(c * rows + cy, cy), :] = out[1]
-        num = fs[0] * out[0] + fs[1] * out[1]
-        den = fs[0] * fs[0] + fs[1] * fs[1]
+
+    @pl.loop(0, nc, unroll=4)
+    def _(c):
+        num, den = 0.0, 0.0
+        for p in range(2):
+            at = pl.ds(c * rows + p * cy, cy)
+            ax = axf[at, :] - outer(0, p, c)
+            axf[at, :] = ax
+            hb[2, p, c] = ax.astype(BF16)
+            num = num + ax * x_ref[at, :]
+            den = den + x_ref[at, :] * x_ref[at, :]
         lbuf[pl.ds(c, 1), :] = jnp.sum(num, axis=0, keepdims=True)
         lbuf[pl.ds(nc + c, 1), :] = jnp.sum(den, axis=0, keepdims=True)
 
+    halo(2, "start")
     lamb[0] = lax.dot_general(
         jnp.ones((8, cz), F32), lbuf[...], (((1,), (1,)), ((), ())),
         precision=lax.Precision.HIGHEST, preferred_element_type=F32)
@@ -210,33 +235,28 @@
 
     for d in range(1, T):
         lam_copy(d).start()
+    halo(1, "start")
     spread(axf, (L.at[3],))
+
+    @pl.loop(0, nc, unroll=4)
+    def _(c):
+        inner(axf, ar_ref, c)
+
     for d in range(1, T):
         lam_copy(d).wait_recv()
     tot = lamb[0]
     for d in range(1, T):
         tot = tot + lamb[d]
+    lams = tot / pltpu.roll(tot, 128 - nc, 1)
 
     for c in range(nc):
-        lam = tot[0:1, c:c + 1] / tot[0:1, nc + c:nc + c + 1]
-        rr = axf[pl.ds(c * rows, rows), :] - lam * x_ref[pl.ds(c * rows, rows), :]
-        rf[pl.ds(c * rows, rows), :] = rr
-        hb[2, 0, c] = rr[:cy].astype(BF16)
-        hb[2, 1, c] = rr[cy:].astype(BF16)
-    halo(2, "start")
+        lam = lams[0:1, c:c + 1]
+        lamr[c] = jnp.broadcast_to(lam, (8, cz))
+        at = pl.ds(c * rows, rows)
+        rf[at, :] = axf[at, :] - lam * x_ref[at, :]
     spread(rf, (W.at[2, v], L.at[1]))
     to_across(2).start()
     to_sib(2).start()
-
-    halo(1, "wait_recv")
-
-    @pl.loop(0, nc)
-    def _(c):
-        _, out = stencil(p_ref, c, 1)
-        axf[pl.ds(c * rows, cy), :] = out[0]
-        axf[pl.ds(c * rows + cy, cy), :] = out[1]
-
-    spread(axf, (L.at[5],))
     to_across(0).wait_recv()
     relay(0).start()
     to_across(1).wait_recv()
@@ -244,13 +264,23 @@
 
     halo(2, "wait_recv")
 
-    @pl.loop(0, nc)
-    def _(c):
-        _, out = stencil(rf, c, 2)
-        ar_ref[pl.ds(c * rows, cy), :] = out[0]
-        ar_ref[pl.ds(c * rows + cy, cy), :] = out[1]
+    @pl.loop(0, nc, unroll=4)
+    def _(c):
+        for p in range(2):
+            at = pl.ds(c * rows + p * cy, cy)
+            ar_ref[at, :] = ar_ref[at, :] - outer(2, p, c) - lamr[c, 0:1, :] * axf[at, :]
 
     spread(ar_ref, (L.at[4],))
+
+    halo(1, "wait_recv")
+
+    @pl.loop(0, nc, unroll=4)
+    def _(c):
+        for p in range(2):
+            at = pl.ds(c * rows + p * cy, cy)
+            apf[at, :] = apf[at, :] - outer(1, p, c)
+
+    spread(apf, (L.at[5],))
 
     def gram(lo, hi):
         def body(k, acc):
@@ -276,11 +306,11 @@
     def reduce(e):
         @pl.when(t < Q)
         def _():
-            total = gpart[e, t]
+            total = gpart[e, t].astype(F32)
             for d in range(1, T):
                 rc(gpart.at[e, 0], grs.at[e, d], rs_s.at[e, d], rs_r.at[e, d], (t + d) % T, v).wait_recv()
-                total = total + grs[e, d]
-            gout[e, t] = total * (1.0 / nvox)
+                total = total + grs[e, d].astype(F32)
+            gout[e, t] = (total * (1.0 / nvox)).astype(BF16)
             for d in range(1, T):
                 ag_copy(e, d, t).start()
 
@@ -290,24 +320,22 @@
     relay(1).wait_recv()
     gx = gram(0, 2)
     for q in range(Q):
-        gpart[0, q] = gx[q * nc:(q + 1) * nc, :]
+        gpart[0, q] = gx[q * nc:(q + 1) * nc, :].astype(BF16)
     rs_each(0, "start")
 
     to_across(2).wait_recv()
     relay(2).start()
     to_sib(2).wait_recv()
-    reduce(0)
     relay(2).wait_recv()
     gr = gram(2, 3)
     pad = jnp.zeros((nc, 4 * nc), F32)
     for q in range(Q):
-        gpart[1, q] = jnp.concatenate([gr[q * nc:(q + 1) * nc, :], pad], axis=1)
+        gpart[1, q] = jnp.concatenate([gr[q * nc:(q + 1) * nc, :], pad], axis=1).astype(BF16)
     rs_each(1, "start")
 
     ct = jnp.concatenate([ct_x, ct_p, ct_r], axis=1)
 
-    @pl.loop(0, nl // CH)
-    def _(k):
+    def advance(k):
         ch = pl.ds(pl.multiple_of(k * CH, CH), CH)
         o = jnp.dot(ct, W[:, :, :, ch].reshape(12 * nc, CH), preferred_element_type=F32)
         for r in range(CH // cz):
@@ -315,19 +343,22 @@
             xo_ref[at, :] = o[:nc, r * cz:(r + 1) * cz]
             po_ref[at, :] = o[nc:, r * cz:(r + 1) * cz]
 
+    pl.loop(0, nl // CH // 2)(advance)
+    reduce(0)
     reduce(1)
+    pl.loop(nl // CH // 2, nl // CH)(advance)
     for e in range(2):
         for q in range(Q):
             @pl.when(t != q)
             def _():
                 ag_copy(e, 1, q).wait_recv()
     n4 = 4 * nc
-    for h in range(2):
+    for h, out in enumerate((gs_ref, ga_ref)):
         for a in range(3):
-            q = 3 * h + a
-            xp = gout[0, q]
-            g_ref[h, a * nc:(a + 1) * nc, :] = jnp.concatenate(
-                [xp[:, :n4], gout[1, q][:, :n4], xp[:, n4:]], axis=1)
+            xp = gout[0, 3 * h + a].astype(F32)
+            out[a, 0] = xp[:, :n4]
+            out[a, 1] = gout[1, 3 * h + a][:, :n4].astype(F32)
+            out[a, 2] = xp[:, n4:]
 
     both(ig_left, ig_right, "wait_send")
     for f in range(3):
@@ -351,13 +382,20 @@
     rows = cx * cy
     nl = rows * cz
     vm = pl.BlockSpec(memory_space=pltpu.VMEM)
+    hbm = pl.BlockSpec(memory_space=pltpu.HBM)
     dma = pltpu.SemaphoreType.DMA
-    xo, po, ar, g = pl.pallas_call(
+    xo, po, ar, gs, ga = pl.pallas_call(
         functools.partial(kernel, T, nc, cy, cz, nl * T),
-        out_shape=[jax.ShapeDtypeStruct((nc * rows, cz), F32)] * 3 + [jax.ShapeDtypeStruct((2, 3 * nc, 12 * nc), F32)],
-        in_specs=[vm, vm, vm, pl.BlockSpec(memory_space=pltpu.SMEM), vm, vm],
-        out_specs=[vm] * 4,
+        out_shape=[jax.ShapeDtypeStruct((nc * rows, cz), F32)] * 3 + [jax.ShapeDtypeStruct((3, 3, nc, 4 * nc), F32)] * 2,
+        in_specs=[hbm, hbm, hbm, pl.BlockSpec(memory_space=pltpu.SMEM), hbm, hbm],
+        out_specs=[vm] * 5,
         scratch_shapes=[
+            pltpu.VMEM((nc * rows, cz), F32),
+            pltpu.VMEM((nc * rows, cz), F32),
+            pltpu.VMEM((cx, cy, cz), F32),
+            pltpu.VMEM(coef_x.shape, BF16),
+            pltpu.VMEM(coef_p.shape, BF16),
+            dma((5,)),
             pltpu.VMEM((2, 2, cy, cz), F32),
             pltpu.VMEM((2, 2, 2, cy, cz), F32),
             pltpu.VMEM((3, 2, nc, cy, cz), BF16),
@@ -367,21 +405,23 @@
             pltpu.VMEM((6, nc, nl), BF16),
             pltpu.VMEM((nc * rows, cz), F32),
             pltpu.VMEM((nc * rows, cz), F32),
+            pltpu.VMEM((nc * rows, cz), F32),
             pltpu.VMEM((128, cz), F32),
             pltpu.VMEM((T, 8, 128), F32),
-            pltpu.VMEM((2, Q, nc, 8 * nc), F32),
-            pltpu.VMEM((2, T, nc, 8 * nc), F32),
-            pltpu.VMEM((2, Q, nc, 8 * nc), F32),
+            pltpu.VMEM((nc, 8, cz), F32),
+            pltpu.VMEM((2, Q, nc, 8 * nc), BF16),
+            pltpu.VMEM((2, T, nc, 8 * nc), BF16),
+            pltpu.VMEM((2, Q, nc, 8 * nc), BF16),
             dma((2,)), dma((2,)), dma((3, 2)), dma((3, 2)), dma((3, 3)), dma((3, 3)),
             dma((T,)), dma((T,)), dma((2, T)), dma((2, T)), dma((2, T)), dma((2, Q)),
         ],
         compiler_params=pltpu.CompilerParams(
-            collective_id=0, has_side_effects=True, vmem_limit_bytes=40 * 1024 * 1024),
+            collective_id=0, has_side_effects=True, vmem_limit_bytes=62 * 1024 * 1024),
     )(vectors.reshape(nc * rows, cz), previous.reshape(nc * rows, cz), intensity, counts, coef_x, coef_p)
     shape = (nc, cx, cy, cz)
     return (
         xo.reshape(shape), po.reshape(shape), ar.reshape(shape),
-        g[0].reshape(3, nc, 3, 4 * nc), g[1].reshape(3, nc, 3, 4 * nc),
+        gs.transpose(0, 2, 1, 3), ga.transpose(0, 2, 1, 3),
     )
 
 

time: 58.4 us -> 52.2 us (0.89)
  Pallas kernels: 48.5 us -> 45 us
  local copies, waits for them, and re-layouts: 8.23 us -> 5.65 us
    pallas_call x1, Pallas kernels: 48.5 us -> 45 us  [shards(): pl.pallas_call(functools.partial(kernel, T, nc, cy, cz, nl * T), out_shap...]
    unnamed x15 -> x13, local copies, waits for them, and re-layouts: 8.04 us -> 5.65 us
where the time goes in v2:
time: 52.2 us; the launch traced here: 51.9 us
  Pallas kernels  45 us (86%)
  local copies, waits for them, and re-layouts  5.65 us (11%)
  between operations  1.3 us (2%)
    pallas_call x1, Pallas kernels, shards(): pl.pallas_call(functools.partial(kernel, T, nc, cy, cz, nl * T), out_shap...  45 us
    unnamed x13, local copies, waits for them, and re-layouts  5.65 us

profile of v2, /device:TPU:0, one launch (start us, length us, event | category | flops | bytes accessed | tf_op | source)
XLA Modules:
  0.0 51.9 jit_solution(12549056583680724995)
XLA Ops:
  1.3 45.0 %shard_map.101 = (f32[1024,128]{1,0:T(8,128)}, f32[1024,128]{1,0:T(8,128)}, f32[1024,128]{1,0:T(8,128)}, f32[3,3,16,64]{3,2,1,0:T(8,128)}, f32[3,3,16,64]{3,2,1,0:T(8,128)}) custom-call(f32[1024,128]{1,0:T(8,128)} %bitcast.7, f32[1024,128]{1,0:T(8,128)} %bitcast.8, f32[2,32,128]{2,1,0:T(8,128)} %int_hbm.1, s32[1]{0:T(128)S(6)} %copy.16.cnt_ref, ...), custom_call_target="tpu_custom_call" | custom-call | tf_op jit(solution)/shard_map/pallas_call | solution.py:387
  46.3 0.0 copy-start.1
  46.3 1.9 %copy.17 = f32[16,2,32,128]{3,2,1,0:T(8,128)} copy(f32[16,2,32,128]{3,2,1,0:T(8,128)} %bitcast.11) | data formatting | bytes 1048576
  48.2 0.0 copy-done.1
  48.2 0.0 copy-start
  48.2 0.8 %copy.18 = f32[16,2,32,128]{3,2,1,0:T(8,128)} copy(f32[16,2,32,128]{3,2,1,0:T(8,128)S(1)} %bitcast.10) | data formatting | bytes 1048576
  49.0 0.4 copy-done
  49.5 0.0 copy-start.3
  49.5 0.8 %copy.19 = f32[16,2,32,128]{3,2,1,0:T(8,128)} copy(f32[16,2,32,128]{3,2,1,0:T(8,128)S(1)} %bitcast.9) | data formatting | bytes 1048576
  50.2 0.1 copy-done.3
  50.4 0.0 copy-start.2
  50.4 0.6 %copy.20 = f32[3,16,3,64]{3,1,2,0:T(8,128)} copy(f32[3,16,3,64]{3,1,2,0:T(8,128)S(1)} %bitcast.13) | data formatting | bytes 73728
  51.0 0.3 copy-done.2
  51.3 0.6 %copy.21 = f32[3,16,3,64]{3,1,2,0:T(8,128)} copy(f32[3,16,3,64]{3,1,2,0:T(8,128)S(1)} %bitcast.12) | data formatting | bytes 73728
Async XLA Ops:
  46.3 2.0 %copy-start.1 = (f32[1024,128]{1,0:T(8,128)S(1)}, f32[1024,128]{1,0:T(8,128)}, u32[]{:S(2)}) copy-start(f32[1024,128]{1,0:T(8,128)} %get-tuple-element.11) | copy-start | bytes 1572868
  48.2 1.2 %copy-start = (f32[1024,128]{1,0:T(8,128)S(1)}, f32[1024,128]{1,0:T(8,128)}, u32[]{:S(2)}) copy-start(f32[1024,128]{1,0:T(8,128)} %get-tuple-element.12) | copy-start | bytes 1572868
  49.5 0.9 %copy-start.3 = (f32[3,3,16,64]{3,2,1,0:T(8,128)S(1)}, f32[3,3,16,64]{3,2,1,0:T(8,128)}, u32[]{:S(2)}) copy-start(f32[3,3,16,64]{3,2,1,0:T(8,128)} %get-tuple-element.13) | copy-start | bytes 110596
  50.4 0.9 %copy-start.2 = (f32[3,3,16,64]{3,2,1,0:T(8,128)S(1)}, f32[3,3,16,64]{3,2,1,0:T(8,128)}, u32[]{:S(2)}) copy-start(f32[3,3,16,64]{3,2,1,0:T(8,128)} %get-tuple-element.14) | copy-start | bytes 110596

commit v3 on v2

--- a/solution.py
+++ b/solution.py
@@ -288,7 +288,7 @@
             a = L[:, :, ch].reshape(6 * nc, CH)
             b = W[lo:hi, :, :, ch].reshape((hi - lo) * 4 * nc, CH)
             return acc + lax.dot_general(a, b, (((1,), (1,)), ((), ())), preferred_element_type=F32)
-        return lax.fori_loop(0, nl // CH, body, jnp.zeros((6 * nc, (hi - lo) * 4 * nc), F32))
+        return lax.fori_loop(0, nl // CH, body, jnp.zeros((6 * nc, (hi - lo) * 4 * nc), F32), unroll=True)
 
     def rs_copy(e, d):
         dst = (t + d) % T
@@ -306,10 +306,10 @@
     def reduce(e):
         @pl.when(t < Q)
         def _():
-            total = gpart[e, t].astype(F32)
+            total = gpart[e, t]
             for d in range(1, T):
                 rc(gpart.at[e, 0], grs.at[e, d], rs_s.at[e, d], rs_r.at[e, d], (t + d) % T, v).wait_recv()
-                total = total + grs[e, d].astype(F32)
+                total = total + grs[e, d]
             gout[e, t] = (total * (1.0 / nvox)).astype(BF16)
             for d in range(1, T):
                 ag_copy(e, d, t).start()
@@ -320,7 +320,7 @@
     relay(1).wait_recv()
     gx = gram(0, 2)
     for q in range(Q):
-        gpart[0, q] = gx[q * nc:(q + 1) * nc, :].astype(BF16)
+        gpart[0, q] = gx[q * nc:(q + 1) * nc, :]
     rs_each(0, "start")
 
     to_across(2).wait_recv()
@@ -330,7 +330,7 @@
     gr = gram(2, 3)
     pad = jnp.zeros((nc, 4 * nc), F32)
     for q in range(Q):
-        gpart[1, q] = jnp.concatenate([gr[q * nc:(q + 1) * nc, :], pad], axis=1).astype(BF16)
+        gpart[1, q] = jnp.concatenate([gr[q * nc:(q + 1) * nc, :], pad], axis=1)
     rs_each(1, "start")
 
     ct = jnp.concatenate([ct_x, ct_p, ct_r], axis=1)
@@ -343,10 +343,10 @@
             xo_ref[at, :] = o[:nc, r * cz:(r + 1) * cz]
             po_ref[at, :] = o[nc:, r * cz:(r + 1) * cz]
 
-    pl.loop(0, nl // CH // 2)(advance)
+    pl.loop(0, nl // CH // 2, unroll=2)(advance)
     reduce(0)
     reduce(1)
-    pl.loop(nl // CH // 2, nl // CH)(advance)
+    pl.loop(nl // CH // 2, nl // CH, unroll=2)(advance)
     for e in range(2):
         for q in range(Q):
             @pl.when(t != q)
@@ -409,14 +409,14 @@
             pltpu.VMEM((128, cz), F32),
             pltpu.VMEM((T, 8, 128), F32),
             pltpu.VMEM((nc, 8, cz), F32),
-            pltpu.VMEM((2, Q, nc, 8 * nc), BF16),
-            pltpu.VMEM((2, T, nc, 8 * nc), BF16),
+            pltpu.VMEM((2, Q, nc, 8 * nc), F32),
+            pltpu.VMEM((2, T, nc, 8 * nc), F32),
             pltpu.VMEM((2, Q, nc, 8 * nc), BF16),
             dma((2,)), dma((2,)), dma((3, 2)), dma((3, 2)), dma((3, 3)), dma((3, 3)),
             dma((T,)), dma((T,)), dma((2, T)), dma((2, T)), dma((2, T)), dma((2, Q)),
         ],
         compiler_params=pltpu.CompilerParams(
-            collective_id=0, has_side_effects=True, vmem_limit_bytes=62 * 1024 * 1024),
+            collective_id=0, has_side_effects=True, vmem_limit_bytes=52 * 1024 * 1024),
     )(vectors.reshape(nc * rows, cz), previous.reshape(nc * rows, cz), intensity, counts, coef_x, coef_p)
     shape = (nc, cx, cy, cz)
     return (

time: 52.2 us -> 50.8 us (0.973)
  Pallas kernels: 45 us -> 43.2 us
    pallas_call x1, Pallas kernels: 45 us -> 43.2 us  [shards(): pl.pallas_call(functools.partial(kernel, T, nc, cy, cz, nl * T), out_shap...]
    unnamed x13 -> x11, local copies, waits for them, and re-layouts: 5.65 us -> 5.95 us
where the time goes in v3:
time: 50.8 us; the launch traced here: 50.4 us
  Pallas kernels  43.2 us (85%)
  local copies, waits for them, and re-layouts  5.95 us (12%)
  between operations  1.3 us (3%)
    pallas_call x1, Pallas kernels, shards(): pl.pallas_call(functools.partial(kernel, T, nc, cy, cz, nl * T), out_shap...  43.2 us
    unnamed x11, local copies, waits for them, and re-layouts  5.95 us

profile of v3, /device:TPU:0, one launch (start us, length us, event | category | flops | bytes accessed | tf_op | source)
XLA Modules:
  0.0 50.4 jit_solution(4897484747790180229)
XLA Ops:
  1.3 0.0 copy-start
  1.3 0.8 %copy-done = bf16[3,64,64]{2,1,0:T(8,128)(2,1)S(1)} copy-done((bf16[3,64,64]{2,1,0:T(8,128)(2,1)S(1)}, bf16[3,64,64]{2,1,0:T(8,128)(2,1)}, u32[]{:S(2)}) %copy-start) | copy-done | bytes 24600
  2.1 0.0 copy-start.1
  2.1 0.8 %copy-done.1 = f32[2,32,128]{2,1,0:T(8,128)S(1)} copy-done((f32[2,32,128]{2,1,0:T(8,128)S(1)}, f32[2,32,128]{2,1,0:T(8,128)}, u32[]{:S(2)}) %copy-start.1) | copy-done | bytes 32792
  2.8 0.0 copy-start.2
  2.8 0.8 %copy-done.2 = bf16[2,64,64]{2,1,0:T(8,128)(2,1)S(1)} copy-done((bf16[2,64,64]{2,1,0:T(8,128)(2,1)S(1)}, bf16[2,64,64]{2,1,0:T(8,128)(2,1)}, u32[]{:S(2)}) %copy-start.2) | copy-done | bytes 16408
  3.6 43.2 %shard_map.101 = (f32[1024,128]{1,0:T(8,128)S(1)}, f32[1024,128]{1,0:T(8,128)S(1)}, f32[1024,128]{1,0:T(8,128)S(1)}, f32[3,3,16,64]{3,2,1,0:T(8,128)S(1)}, f32[3,3,16,64]{3,2,1,0:T(8,128)S(1)}) custom-call(f32[1024,128]{1,0:T(8,128)} %bitcast.12, f32[1024,128]{1,0:T(8,128)} %bitcast.13, f32[2,32,128]{2,1,0:T(8,128)S(1)} %copy-done.1, s32[1]{0:T(128)S(6)} %copy.16.cnt_ref, ...), custom_call_target="tpu_custom_call" | custom-call | tf_op jit(solution)/shard_map/pallas_call | solution.py:387
  46.8 0.8 %copy.17 = f32[16,2,32,128]{3,2,1,0:T(8,128)} copy(f32[16,2,32,128]{3,2,1,0:T(8,128)S(1)} %bitcast.9) | data formatting | bytes 1048576
  47.6 0.8 %copy.18 = f32[16,2,32,128]{3,2,1,0:T(8,128)} copy(f32[16,2,32,128]{3,2,1,0:T(8,128)S(1)} %bitcast.8) | data formatting | bytes 1048576
  48.4 0.8 %copy.19 = f32[16,2,32,128]{3,2,1,0:T(8,128)} copy(f32[16,2,32,128]{3,2,1,0:T(8,128)S(1)} %bitcast.7) | data formatting | bytes 1048576
  49.2 0.6 %copy.20 = f32[3,16,3,64]{3,1,2,0:T(8,128)} copy(f32[3,16,3,64]{3,1,2,0:T(8,128)S(1)} %bitcast.11) | data formatting | bytes 73728
  49.8 0.6 %copy.21 = f32[3,16,3,64]{3,1,2,0:T(8,128)} copy(f32[3,16,3,64]{3,1,2,0:T(8,128)S(1)} %bitcast.10) | data formatting | bytes 73728
Async XLA Ops:
  1.3 0.8 %copy-start = (bf16[3,64,64]{2,1,0:T(8,128)(2,1)S(1)}, bf16[3,64,64]{2,1,0:T(8,128)(2,1)}, u32[]{:S(2)}) copy-start(bf16[3,64,64]{2,1,0:T(8,128)(2,1)} %cfx_hbm.1) | copy-start | bytes 73732
  2.1 0.8 %copy-start.1 = (f32[2,32,128]{2,1,0:T(8,128)S(1)}, f32[2,32,128]{2,1,0:T(8,128)}, u32[]{:S(2)}) copy-start(f32[2,32,128]{2,1,0:T(8,128)} %int_hbm.1) | copy-start | bytes 98308
  2.8 0.8 %copy-start.2 = (bf16[2,64,64]{2,1,0:T(8,128)(2,1)S(1)}, bf16[2,64,64]{2,1,0:T(8,128)(2,1)}, u32[]{:S(2)}) copy-start(bf16[2,64,64]{2,1,0:T(8,128)(2,1)} %cfp_hbm.1) | copy-start | bytes 49156
